TPU v7x, 32 devices: a whole 2x2x4 slice. The times are simulated.
32 devices in a mesh: fg: 4 (over y, core), sp: 8 (over z, x).
Axes of the slice: x: 2, y: 2, z: 4, core: 2. Of those that a mesh axis runs over, the one named last changes fastest.
Arguments:
- latent: bfloat16 [16, 64, 240, 256], P('fg', 'sp'), may hold values from -6 to 6
- temporal_weight: bfloat16 [3, 256, 1024], replicated, may hold values from -0.21875 to 0.21875
- temporal_bias: float32 [1024], replicated, may hold values from -4 to 4
- spatial_weight: bfloat16 [3, 3, 256, 128], replicated, may hold values from -0.125 to 0.125
- spatial_bias: float32 [128], replicated, may hold values from -4 to 4
- counts: int32 [4], replicated, may hold values from 1 to 16, 48 in all
Outputs:
- decoded: bfloat16 [64, 64, 240, 128], P('fg', 'sp')
Inputs may be any that keep to these rules, and one draw needn't show every extreme that they name: `counts`: some group holds 16.
All inputs are finite; a program needn't handle non-finite values.
Results may differ from a plain program's by a relative error of at most 0.0038.
Values may be sent and summed in bfloat16 or wider, within the bound.
A program may use at most 320 MiB of HBM per device.

v0:
```python
import jax
import jax.numpy as jnp
from jax import lax
from jax.sharding import PartitionSpec as P


def shifted(x, axis, by):
    size = lax.axis_size(axis)
    pairs = [(i, i + by) for i in range(size) if 0 <= i + by < size]
    return lax.ppermute(x, axis, pairs)


def extended(x, sides, width):
    for axis, dim in sides:
        size, length = (lax.axis_size(axis), x.shape[dim])
        up = [(i, (i + 1) % size) for i in range(size - 1)]
        down = [(j, i) for i, j in up]
        last = lax.slice_in_dim(x, length - width, length, axis=dim)
        leading = lax.slice_in_dim(x, 0, width, axis=dim)
        before = lax.ppermute(last, axis, up)
        after = lax.ppermute(leading, axis, down)
        x = jnp.concatenate([before, x, after], axis=dim)
    return x


def spatial_taps(framed, spatial_weight, spatial_bias, rows, cols):
    total = jnp.zeros((framed.shape[0], rows, cols, spatial_weight.shape[3]), jnp.float32)
    for dy in range(3):
        for dx in range(3):
            total = total + jnp.einsum(
                "fhwc,cd->fhwd",
                framed[:, dy : dy + rows, dx : dx + cols, :],
                spatial_weight[dy, dx],
                preferred_element_type=jnp.float32,
            )
    return (total + spatial_bias).astype(jnp.bfloat16)


def temporal_block(padded, temporal_weight, temporal_bias, local_frames):
    rows, cols, width = (padded.shape[1], padded.shape[2], padded.shape[3])
    pre = jnp.zeros((local_frames, 4, rows, cols, width), jnp.float32)
    for tap in range(3):
        kernel = temporal_weight[tap].reshape(width, 4, width)
        pre = pre + jnp.einsum(
            "lhwc,cjd->ljhwd",
            padded[tap : tap + local_frames],
            kernel,
            preferred_element_type=jnp.float32,
        )
    pre = pre + temporal_bias.reshape(1, 4, 1, 1, width)
    return jax.nn.silu(pre).astype(jnp.bfloat16).reshape(4 * local_frames, rows, cols, width)


def on_device(latent, temporal_weight, temporal_bias, spatial_weight, spatial_bias, counts):
    local_frames, rows, cols, width = latent.shape
    edge = shifted(latent[local_frames - 2 :], "fg", 1)
    padded = jnp.concatenate([edge, latent], axis=0)
    upper = temporal_block(padded, temporal_weight, temporal_bias, local_frames)
    rimmed = extended(upper, (("sp", 1),), 1)
    framed = jnp.pad(rimmed, ((0, 0), (0, 0), (1, 1), (0, 0)))
    result = spatial_taps(framed, spatial_weight, spatial_bias, rows, cols)
    group = lax.axis_index("fg")
    groups = jnp.arange(counts.shape[0], dtype=jnp.int32)
    limit = jnp.sum(jnp.where(groups == group, counts, 0))
    positions = jnp.arange(4 * local_frames, dtype=jnp.int32)
    valid = (positions < limit).astype(jnp.bfloat16).reshape(4 * local_frames, 1, 1, 1)
    return result * valid


def solution(mesh):
    return jax.shard_map(
        on_device,
        mesh=mesh,
        in_specs=(P("fg", "sp", None, None), P(), P(), P(), P(), P()),
        out_specs=P("fg", "sp", None, None),
        check_vma=False,
    )
```

profile of v0, /device:TPU:25, one launch (start us, length us, event | category | flops | bytes accessed | tf_op | source)
XLA Modules:
  0.0 338.4 jit_solution(16131108231490050728)
XLA Ops:
  0.0 2.9 slice.81
  2.9 3.7 %collective-permute-start = (bf16[2,8,240,256]{3,2,1,0:T(8,128)(2,1)}, bf16[2,8,240,256]{3,2,1,0:T(8,128)(2,1)S(1)}, u32[]{:S(2)}, u32[]{:S(2)}) collective-permute-start(bf16[2,8,240,256]{3,2,1,0:T(8,128)(2,1)} %slice.81), channel_id=1, source_target_pairs={{0,8},{8,16},{16,24},{1,9},{9,17},{17,25},{2,10},{10,18},{18,26},{... | collective-permute-start | bytes 5898248 | tf_op jit(solution)/shard_map/ppermute | solution.py:10
  6.7 0.7 add.60
  7.3 1.5 fusion.58
  8.8 1.0 copy.35
  9.8 0.2 copy.36
  10.0 0.2 copy.37
  10.3 0.0 copy-start.1
  10.3 14.8 %fusion.29 = f32[4,256,4,8,240]{1,4,0,3,2:T(8,128)} fusion(bf16[256,4,256,1,1]{0,2,1,4,3:T(8,128)(2,1)S(1)} %bitcast.113, bf16[4,8,240,256]{3,2,1,0:T(8,128)(2,1)} %param.6), kind=kOutput, calls=%fused_computation.36 | convolution fusion | flops 4026531840 | bytes 35913728 | tf_op jit(solution)/shard_map/lhwc,cjd->ljhwd/dot_general | solution.py:44
  25.1 3.4 %collective-permute-done = bf16[2,8,240,256]{3,2,1,0:T(8,128)(2,1)S(1)} collective-permute-done((bf16[2,8,240,256]{3,2,1,0:T(8,128)(2,1)}, bf16[2,8,240,256]{3,2,1,0:T(8,128)(2,1)S(1)}, u32[]{:S(2)}, u32[]{:S(2)}) %collective-permute-start) | collective-permute-done | bytes 1966112 | tf_op jit(solution)/shard_map/ppermute | solution.py:10
  28.5 0.1 constant_dynamic-update-slice_fusion.1
  28.7 0.3 constant_dynamic-update-slice_fusion
  29.0 12.4 %fusion.28 = f32[4,8,240,4,256]{4,2,3,1,0:T(8,128)} fusion(bf16[256,4,256,1,1]{0,2,1,4,3:T(8,128)(2,1)S(1)} %bitcast.112, bf16[6,8,240,256]{3,2,1,0:T(8,128)(2,1)S(1)} %constant_dynamic-update-slice_fusion), kind=kOutput, calls=%fused_computation.34 | convolution fusion | flops 4026531840 | bytes 35913728 | tf_op jit(solution)/shard_map/lhwc,cjd->ljhwd/dot_general | solution.py:44
  41.4 28.7 %multiply_convert_fusion = bf16[4,4,8,240,256]{4,3,1,2,0:T(8,128)(2,1)} fusion(f32[4,256,4,8,240]{1,4,0,3,2:T(8,128)} %fusion.29, f32[4,8,240,4,256]{4,2,3,1,0:T(8,128)} %fusion.28, f32[4,256]{1,0:T(4,128)S(1)} %add.60, bf16[256,4,256,1,1]{0,2,1,4,3:T(8,128)(2,1)S(1)} %bitcast.114, bf16[6,8,240,256]{3,2,1,0:T(8,128)(2,1)} %copy-done.2), kind=kOutput, calls=%fused_computation.5 | convolution fusion | flops 4089446400 | bytes 83103744 | tf_op jit(solution)/shard_map/lhwc,cjd->ljhwd/dot_general | solution.py:44
  70.0 7.8 %copy.15 = bf16[4,4,8,240,256]{4,3,2,1,0:T(8,128)(2,1)S(1)} copy(bf16[4,4,8,240,256]{4,3,1,2,0:T(8,128)(2,1)} %multiply_convert_fusion) | data formatting | bytes 31457280 | tf_op jit(solution)/shard_map/convert_element_type | solution.py:51
  77.9 2.4 fusion.57
  80.3 3.1 collective-permute-start.1
  83.4 3.3 collective-permute-start.2
  86.7 0.6 fusion.54
  87.4 0.6 compare_convert_fusion
  88.0 7.7 %fusion.39 = f32[16,8,240,128]{3,2,1,0:T(8,128)} fusion(bf16[16,8,240,256]{3,2,1,0:T(8,128)(2,1)S(1)} %bitcast.108, bf16[3,3,256,128]{3,2,1,0:T(8,128)(2,1)S(1)} %copy-done.4), kind=kOutput, calls=%fused_computation.42 | convolution fusion | flops 2013265920 | bytes 31522816 | tf_op jit(solution)/shard_map/fhwc,cd->fhwd/dot_general | solution.py:30
  95.7 28.0 %collective-permute-done.1 = bf16[16,1,240,256]{3,2,1,0:T(8,128)(2,1)S(1)} collective-permute-done((bf16[16,1,240,256]{3,2,1,0:T(8,128)(2,1)}, bf16[16,1,240,256]{3,2,1,0:T(8,128)(2,1)S(1)}, u32[]{:S(2)}, u32[]{:S(2)}) %collective-permute-start.1) | collective-permute-done | bytes 1966112 | tf_op jit(solution)/shard_map/ppermute | solution.py:20
  123.8 42.2 %collective-permute-done.2 = bf16[16,1,240,256]{3,2,1,0:T(8,128)(2,1)S(1)} collective-permute-done((bf16[16,1,240,256]{3,2,1,0:T(8,128)(2,1)}, bf16[16,1,240,256]{3,2,1,0:T(8,128)(2,1)S(1)}, u32[]{:S(2)}, u32[]{:S(2)}) %collective-permute-start.2) | collective-permute-done | bytes 1966112 | tf_op jit(solution)/shard_map/ppermute | solution.py:21
  166.0 17.5 %fusion.6 = bf16[16,10,242,256]{3,2,1,0:T(8,128)(2,1)} fusion(bf16[16,1,240,256]{3,2,1,0:T(8,128)(2,1)S(1)} %collective-permute-done.2, bf16[16,8,240,256]{3,2,1,0:T(8,128)(2,1)S(1)} %bitcast.109, bf16[16,1,240,256]{3,2,1,0:T(8,128)(2,1)S(1)} %collective-permute-done.1), kind=kLoop, calls=%fused_computation.10 | loop fusion | flops 118947840 | bytes 39485440 | tf_op jit(solution)/shard_map/concatenate | solution.py:22
  183.5 15.3 %fusion.17 = f32[16,8,240,128]{3,2,1,0:T(8,128)} fusion(bf16[16,10,242,256]{3,2,1,0:T(8,128)(2,1)} %fusion.6, bf16[3,3,256,128]{3,2,1,0:T(8,128)(2,1)S(1)} %copy-done.4), kind=kOutput, calls=%fused_computation.21 | convolution fusion | flops 2013265920 | bytes 31522816 | tf_op jit(solution)/shard_map/fhwc,cd->fhwd/dot_general | solution.py:30
  198.8 15.4 %fusion.19 = f32[16,8,240,128]{3,2,1,0:T(8,128)} fusion(bf16[16,10,242,256]{3,2,1,0:T(8,128)(2,1)} %fusion.6, bf16[3,3,256,128]{3,2,1,0:T(8,128)(2,1)S(1)} %copy-done.4), kind=kOutput, calls=%fused_computation.23 | convolution fusion | flops 2013265920 | bytes 31522816 | tf_op jit(solution)/shard_map/fhwc,cd->fhwd/dot_general | solution.py:30
  214.2 15.2 %fusion.21 = f32[16,8,240,128]{3,2,1,0:T(8,128)} fusion(bf16[16,10,242,256]{3,2,1,0:T(8,128)(2,1)} %fusion.6, bf16[3,3,256,128]{3,2,1,0:T(8,128)(2,1)S(1)} %copy-done.4), kind=kOutput, calls=%fused_computation.25 | convolution fusion | flops 2013265920 | bytes 31522816 | tf_op jit(solution)/shard_map/fhwc,cd->fhwd/dot_general | solution.py:30
  229.4 25.0 %fusion.23 = f32[16,8,240,128]{3,2,1,0:T(8,128)} fusion(bf16[16,10,242,256]{3,2,1,0:T(8,128)(2,1)} %fusion.6, bf16[3,3,256,128]{3,2,1,0:T(8,128)(2,1)S(1)} %copy-done.4), kind=kOutput, calls=%fused_computation.27 | convolution fusion | flops 2013265920 | bytes 31522816 | tf_op jit(solution)/shard_map/fhwc,cd->fhwd/dot_general | solution.py:30
  254.4 15.3 %fusion.25 = f32[16,8,240,128]{3,2,1,0:T(8,128)} fusion(bf16[16,10,242,256]{3,2,1,0:T(8,128)(2,1)} %fusion.6, bf16[3,3,256,128]{3,2,1,0:T(8,128)(2,1)S(1)} %copy-done.4), kind=kOutput, calls=%fused_computation.29 | convolution fusion | flops 2013265920 | bytes 31522816 | tf_op jit(solution)/shard_map/fhwc,cd->fhwd/dot_general | solution.py:30
  269.7 10.6 %fusion.11 = f32[16,8,240,128]{3,2,1,0:T(8,128)} fusion(bf16[16,1,240,256]{3,2,1,0:T(8,128)(2,1)S(1)} %collective-permute-done.2, bf16[16,8,240,256]{3,2,1,0:T(8,128)(2,1)} %bitcast.110, bf16[3,3,256,128]{3,2,1,0:T(8,128)(2,1)S(1)} %copy-done.4), kind=kOutput, calls=%fused_computation.15 | convolution fusion | flops 2048655360 | bytes 33488896 | tf_op jit(solution)/shard_map/fhwc,cd->fhwd/dot_general | solution.py:30
  280.3 10.7 %fusion.7 = f32[16,8,240,128]{3,2,1,0:T(8,128)} fusion(bf16[16,8,240,256]{3,2,1,0:T(8,128)(2,1)} %bitcast.111, bf16[16,1,240,256]{3,2,1,0:T(8,128)(2,1)S(1)} %collective-permute-done.1, bf16[3,3,256,128]{3,2,1,0:T(8,128)(2,1)S(1)} %copy-done.4), kind=kOutput, calls=%fused_computation.11 | convolution fusion | flops 2048655360 | bytes 33488896 | tf_op jit(solution)/shard_map/fhwc,cd->fhwd/dot_general | solution.py:30
  291.0 47.2 %fusion.27 = bf16[16,8,240,128]{3,2,1,0:T(8,128)(2,1)} fusion(f32[128]{0:T(128)S(1)} %copy-done.5, f32[16,8,240,128]{3,2,1,0:T(8,128)} %fusion.11, f32[16,8,240,128]{3,2,1,0:T(8,128)} %fusion.17, f32[16,8,240,128]{3,2,1,0:T(8,128)} %fusion.19, f32[16,8,240,128]{3,2,1,0:T(8,128)} %fusion.39, f32[16,8,240,128]{3,2,1,0:T(8,128)} %fusion.21, ...), kind=kOutput, calls=%fused_computation.32 | convolution fusion | flops 2056519680 | bytes 149488640 | tf_op jit(solution)/shard_map/fhwc,cd->fhwd/dot_general | solution.py:30
  (13 shorter events, 0.0 us)
Async XLA Ops:
  2.9 25.6 %collective-permute-start = (bf16[2,8,240,256]{3,2,1,0:T(8,128)(2,1)}, bf16[2,8,240,256]{3,2,1,0:T(8,128)(2,1)S(1)}, u32[]{:S(2)}, u32[]{:S(2)}) collective-permute-start(bf16[2,8,240,256]{3,2,1,0:T(8,128)(2,1)} %slice.81), channel_id=1, source_target_pairs={{0,8},{8,16},{16,24},{1,9},{9,17},{17,25},{2,10},{10,18},{18,26},{... | collective-permute-start | bytes 5898248 | tf_op jit(solution)/shard_map/ppermute | solution.py:10
  10.3 18.4 %copy-start.1 = (bf16[4,8,240,256]{3,2,1,0:T(8,128)(2,1)S(1)}, bf16[4,8,240,256]{3,2,1,0:T(8,128)(2,1)}, u32[]{:S(2)}) copy-start(bf16[4,8,240,256]{3,2,1,0:T(8,128)(2,1)} %param.6) | copy-start | bytes 11796484
  29.0 12.4 %copy-start.2 = (bf16[6,8,240,256]{3,2,1,0:T(8,128)(2,1)}, bf16[6,8,240,256]{3,2,1,0:T(8,128)(2,1)S(1)}, u32[]{:S(2)}) copy-start(bf16[6,8,240,256]{3,2,1,0:T(8,128)(2,1)S(1)} %constant_dynamic-update-slice_fusion) | copy-start | bytes 17694724
  29.0 12.4 %copy-start.3 = (bf16[1,256,1024]{1,2,0:T(8,128)(2,1)S(1)}, bf16[1,256,1024]{1,2,0:T(8,128)(2,1)}, u32[]{:S(2)}) copy-start(bf16[1,256,1024]{1,2,0:T(8,128)(2,1)} %copy.35) | copy-start | bytes 1572868
  70.0 16.7 %copy-start.6 = (s32[4]{0:T(128)S(1)}, s32[4]{0:T(128)}, u32[]{:S(2)}) copy-start(s32[4]{0:T(128)} %param.11) | copy-start | bytes 52
  70.0 17.9 %copy-start.4 = (bf16[3,3,256,128]{3,2,1,0:T(8,128)(2,1)S(1)}, bf16[3,3,256,128]{3,2,1,0:T(8,128)(2,1)}, u32[]{:S(2)}) copy-start(bf16[3,3,256,128]{3,2,1,0:T(8,128)(2,1)} %param.9) | copy-start | bytes 1769476
  77.8 88.2 %copy-start = (bf16[4,4,8,240,256]{4,3,2,1,0:T(8,128)(2,1)}, bf16[4,4,8,240,256]{4,3,2,1,0:T(8,128)(2,1)S(1)}, u32[]{:S(2)}) copy-start(bf16[4,4,8,240,256]{4,3,2,1,0:T(8,128)(2,1)S(1)} %copy.15) | copy-start | bytes 47185924
  80.3 43.5 %collective-permute-start.1 = (bf16[16,1,240,256]{3,2,1,0:T(8,128)(2,1)}, bf16[16,1,240,256]{3,2,1,0:T(8,128)(2,1)S(1)}, u32[]{:S(2)}, u32[]{:S(2)}) collective-permute-start(bf16[16,1,240,256]{3,2,1,0:T(8,128)(2,1)} %get-tuple-element.5), channel_id=1, source_target_pairs={{0,1},{1,2},{2,3},{3,4},{4,5},{5,6},{6,7},{8,9},{9,10},{10,11},{11... | collective-permute-start | bytes 5898248 | tf_op jit(solution)/shard_map/ppermute | solution.py:20
  83.4 82.6 %collective-permute-start.2 = (bf16[16,1,240,256]{3,2,1,0:T(8,128)(2,1)}, bf16[16,1,240,256]{3,2,1,0:T(8,128)(2,1)S(1)}, u32[]{:S(2)}, u32[]{:S(2)}) collective-permute-start(bf16[16,1,240,256]{3,2,1,0:T(8,128)(2,1)} %get-tuple-element.6), channel_id=1, source_target_pairs={{1,0},{2,1},{3,2},{4,3},{5,4},{6,5},{7,6},{9,8},{10,9},{11,10},{12... | collective-permute-start | bytes 5898248 | tf_op jit(solution)/shard_map/ppermute | solution.py:21
  280.3 10.7 %copy-start.5 = (f32[128]{0:T(128)S(1)}, f32[128]{0:T(128)}, u32[]{:S(2)}) copy-start(f32[128]{0:T(128)} %param.10) | copy-start | bytes 1540
where the time goes:
time: 341 us; the launch traced here: 338 us
  matrix products  218 us (64%)
  waiting for transfers between devices  73.7 us (22%)
  other arithmetic  18.8 us (6%)
  local copies, waits for them, and re-layouts  17.2 us (5%)
  starting transfers between devices  10.1 us (3%)
    dot_general x9, matrix products, spatial_taps(): jnp.einsum('fhwc,cd->fhwd', framed[:, dy:dy + rows, dx:dx + cols, :], spa...  162 us
    dot_general x3, matrix products, temporal_block(): jnp.einsum('lhwc,cjd->ljhwd', padded[tap:tap + local_frames], kernel, pre...  55.9 us
    ppermute x1, waiting for transfers between devices, extended(): after = lax.ppermute(leading, axis, down)  42.2 us
    ppermute x1, waiting for transfers between devices, extended(): before = lax.ppermute(last, axis, up)  28 us
    concatenate x1, other arithmetic, extended(): x = jnp.concatenate([before, x, after], axis=dim)  17.5 us
    convert_element_type x1, local copies, waits for them, and re-layouts, temporal_block(): jax.nn.silu(pre).astype(jnp.bfloat16)  7.79 us
  transfers between devices with their start and end apart: 3, of which 3 were waited for; matrix products, arithmetic and copies ran while one was open for 8% of the time, Pallas kernels for 0%

commit v1 on v0

v1 whole, which is shorter than its diff:
```python
import functools

import jax
import jax.numpy as jnp
from jax import lax
from jax.experimental import pallas as pl
from jax.experimental.pallas import tpu as pltpu
from jax.sharding import PartitionSpec as P

F32, BF16 = jnp.float32, jnp.bfloat16
LIMIT = 58 * 1024 * 1024
MESH = pl.DeviceIdType.MESH
SENDS = ((0, 1), (0, -1), (1, 1), (1, -1), (1, 0))
NEIGHBOURS = tuple((f, s) for f in (-1, 0, 1) for s in (-1, 0, 1) if f or s)


def silu(pre):
    half = 0.5 * pre
    return half + half * jnp.tanh(half)


def fill_weights(sw_ref, w01, w2):
    depth, wide = sw_ref.shape[2], sw_ref.shape[3]
    zero = jnp.zeros((depth, wide), BF16)
    for dy in range(3):
        at = pl.ds(dy * depth, depth)
        w01[at, :wide] = sw_ref[dy, 0]
        w01[at, wide:] = sw_ref[dy, 1]
    for q in range(4):
        at = pl.ds(q * depth, depth)
        w2[at, :wide] = sw_ref[q, 2] if q < 3 else zero
        w2[at, wide:] = sw_ref[q - 1, 2] if q > 0 else zero


def activation(a, j, tw_ref, tb_ref):
    width = tw_ref.shape[1] // 4
    columns = pl.ds(pl.multiple_of(j * width, width), width)
    pre = jnp.dot(a, tw_ref[:, columns], preferred_element_type=F32) + tb_ref[:, columns]
    return silu(pre).astype(BF16)


def zero_rims(left, right, cols):
    n, _, wide = left.shape
    left[:, 0:8, :] = jnp.zeros((n, 8, wide), F32)
    right[:, cols:cols + 8, :] = jnp.zeros((n, 8, wide), F32)


def row_pair(row, cols, w01, w2, left, right, sb_ref, p):
    wide = sb_ref.shape[1]
    taps = [row(q) for q in range(4)]
    a = jnp.concatenate([jnp.concatenate(taps[h:h + 3], axis=1) for h in range(2)], axis=0)
    r = jnp.dot(a, w01[...], preferred_element_type=F32)
    s = jnp.dot(jnp.concatenate(taps, axis=1), w2[...], preferred_element_type=F32)
    rows = []
    for h in range(2):
        left[2 * p + h, 8:8 + cols, :] = r[h * cols:(h + 1) * cols, :wide]
        right[2 * p + h, 0:cols, :] = s[:, h * wide:(h + 1) * wide]
        middle = r[h * cols:(h + 1) * cols, wide:] + sb_ref[...]
        rows.append((left[2 * p + h, 7:7 + cols, :] + middle + right[2 * p + h, 1:1 + cols, :]).astype(BF16))
    return rows


def late_kernel(sizes, latent_ref, tw_ref, tb_ref, sw_ref, sb_ref, out_ref, halo_ref, edge_ref,
                lat, up, w01, w2, w3, left, right, load_sem, send_sem, recv_sem):
    frames, rows, cols, width = latent_ref.shape
    wide = sb_ref.shape[1]
    fg, sp = lax.axis_index("fg"), lax.axis_index("sp")

    loads = [pltpu.make_async_copy(latent_ref.at[f], lat.at[f], load_sem.at[f]) for f in range(frames)]
    for load in loads:
        load.start()

    def there(by, back=False):
        f, s = (fg - by[0], sp - by[1]) if back else (fg + by[0], sp + by[1])
        return (f >= 0) & (f < sizes[0]) & (s >= 0) & (s < sizes[1])

    barrier = pltpu.get_barrier_semaphore()
    for by in NEIGHBOURS:
        @pl.when(there(by))
        def _():
            pl.semaphore_signal(barrier, inc=1, device_id=(fg + by[0], sp + by[1]), device_id_type=MESH)
    near = [1 + (at > 0).astype(jnp.int32) + (at < n - 1).astype(jnp.int32) for at, n in zip((fg, sp), sizes)]
    pl.semaphore_wait(barrier, near[0] * near[1] - 1)

    last, head = latent_ref.at[:, rows - 1], latent_ref.at[:, 0]
    tail = pl.ds(frames - 2, 2)
    sources = (last, head, latent_ref.at[tail, rows - 1], latent_ref.at[tail, 0], latent_ref.at[tail])
    own, corner = pl.ds(2, frames), pl.ds(0, 2)
    targets = (halo_ref.at[0, own], halo_ref.at[1, own], halo_ref.at[0, corner], halo_ref.at[1, corner], edge_ref)

    def sent(i):
        by = SENDS[i]
        return pltpu.make_async_remote_copy(
            src_ref=sources[i], dst_ref=targets[i], send_sem=send_sem.at[i], recv_sem=recv_sem.at[i],
            device_id=(fg + by[0], sp + by[1]), device_id_type=MESH,
        )

    for i, by in enumerate(SENDS):
        @pl.when(there(by))
        def _():
            sent(i).start()

    fill_weights(sw_ref, w01, w2)
    for dy in range(3):
        for dx in range(3):
            w3[dy * width:(dy + 1) * width, dx * wide:(dx + 1) * wide] = sw_ref[dy, dx]
    zero_rims(left, right, cols)
    for load in loads:
        load.wait()

    def inner(i, carry):
        l, j = i // 4, i % 4
        a = jnp.concatenate([lat[l + k].reshape(rows * cols, width) for k in range(3)], axis=1)
        up[i] = activation(a, j, tw_ref, tb_ref)
        for p in range(rows // 2 - 1):
            row = lambda q: up[i, pl.ds((2 * p + q) * cols, cols), :]
            for h, value in enumerate(row_pair(row, cols, w01, w2, left, right, sb_ref, p)):
                out_ref[i, 2 * p + 1 + h] = value
        return carry

    lax.fori_loop(0, 8, inner, 0)

    for i in range(2):
        @pl.when(there(SENDS[i], True))
        def _():
            sent(i).wait_recv()

    def rim(i, carry):
        l, j = i // 4, i % 4
        a = jnp.concatenate([halo_ref[:, 2 + l + k].reshape(2 * cols, width) for k in range(3)], axis=1)
        act = activation(a, j, tw_ref, tb_ref)
        zero = jnp.zeros((cols, width), BF16)
        row = lambda h: up[i, pl.ds(h * cols, cols), :]
        above = [jnp.where(sp > 0, act[:cols], zero), row(0), row(1)]
        below = [row(rows - 2), row(rows - 1), jnp.where(sp < sizes[1] - 1, act[cols:], zero)]
        a = jnp.concatenate([jnp.concatenate(above, axis=1), jnp.concatenate(below, axis=1)], axis=0)
        r = jnp.dot(a, w3[...], preferred_element_type=F32)
        for h in range(2):
            part = r[h * cols:(h + 1) * cols]
            left[h, 8:8 + cols, :] = part[:, :wide]
            right[h, 0:cols, :] = part[:, 2 * wide:]
            total = left[h, 7:7 + cols, :] + (part[:, wide:2 * wide] + sb_ref[...]) + right[h, 1:1 + cols, :]
            out_ref[i, h * (rows - 1)] = total.astype(BF16)
        return carry

    lax.fori_loop(0, 8, rim, 0)

    for i, by in enumerate(SENDS):
        if i >= 2:
            @pl.when(there(by, True))
            def _():
                sent(i).wait_recv()

        @pl.when(there(by))
        def _():
            sent(i).wait_send()


def late_call(sizes, latent, tw, tb, sw, sb):
    frames, rows, cols, width = latent.shape
    wide = sw.shape[3]
    vmem = pl.BlockSpec(memory_space=pltpu.VMEM)
    hbm = pl.BlockSpec(memory_space=pl.ANY)
    return pl.pallas_call(
        functools.partial(late_kernel, sizes),
        in_specs=[hbm] + [vmem] * 4,
        out_specs=[vmem, vmem, hbm],
        out_shape=[
            jax.ShapeDtypeStruct((8, rows, cols, wide), BF16),
            jax.ShapeDtypeStruct((2, frames + 2, cols, width), BF16),
            jax.ShapeDtypeStruct((2, rows, cols, width), BF16),
        ],
        scratch_shapes=[
            pltpu.VMEM((frames, rows, cols, width), BF16),
            pltpu.VMEM((8, rows * cols, width), BF16),
            pltpu.VMEM((3 * width, 2 * wide), BF16),
            pltpu.VMEM((4 * width, 2 * wide), BF16),
            pltpu.VMEM((3 * width, 3 * wide), BF16),
            pltpu.VMEM((rows, cols + 8, wide), F32),
            pltpu.VMEM((rows, cols + 8, wide), F32),
            pltpu.SemaphoreType.DMA((frames,)),
            pltpu.SemaphoreType.DMA((len(SENDS),)),
            pltpu.SemaphoreType.DMA((len(SENDS),)),
        ],
        compiler_params=pltpu.CompilerParams(
            collective_id=0, has_side_effects=True, vmem_limit_bytes=LIMIT
        ),
        cost_estimate=pl.CostEstimate(flops=18 * 10**9, bytes_accessed=16 * 10**6, transcendentals=5 * 10**6),
        name="late_frames",
    )(latent, tw, tb, sw, sb)


def early_kernel(counts_ref, edge_ref, latent_ref, halo_ref, late_ref, tw_ref, tb_ref, sw_ref, sb_ref, out_ref,
                 x_ref, up, w01, w2, left, right):
    rows, cols, width = latent_ref.shape[1:]
    fg, sp = lax.axis_index("fg"), lax.axis_index("sp")
    last_sp = lax.axis_size("sp") - 1
    l, j = pl.program_id(0), pl.program_id(1)
    step = 4 * l + j

    @pl.when(step == 0)
    def _():
        fill_weights(sw_ref, w01, w2)
        zero_rims(left, right, cols)

    def put(k, at, frame):
        x_ref[at * cols:at * cols + frame.shape[0], k * width:(k + 1) * width] = frame

    for at in range(2):
        @pl.when((l == at) & (j == 0))
        def _():
            for k in range(3):
                source = at + k - 2
                top, bottom = halo_ref[0, source + 2], halo_ref[1, source + 2]
                if source < 0:
                    body = edge_ref[source + 2].reshape(rows * cols, width)
                    top, body, bottom = (jnp.where(fg > 0, a, jnp.zeros_like(a)) for a in (top, body, bottom))
                else:
                    body = latent_ref[source].reshape(rows * cols, width)
                put(k, 0, top)
                put(k, 1, body)
                put(k, rows + 1, bottom)

    limit = counts_ref[fg]
    valid = step < limit

    @pl.when(valid)
    def _():
        up[...] = activation(x_ref[...], j, tw_ref, tb_ref)

        @pl.when(sp == 0)
        def _():
            up[0:cols, :] = jnp.zeros((cols, width), BF16)

        @pl.when(sp == last_sp)
        def _():
            up[(rows + 1) * cols:, :] = jnp.zeros((cols, width), BF16)

        for p in range(rows // 2):
            row = lambda q: up[pl.ds((2 * p + q) * cols, cols), :]
            for h, value in enumerate(row_pair(row, cols, w01, w2, left, right, sb_ref, p)):
                out_ref[0, 0, 2 * p + h] = value

    @pl.when(jnp.logical_not(valid))
    def _():
        out_ref[0] = jnp.zeros(out_ref.shape[1:], BF16)

    @pl.when(step + 8 < limit)
    def _():
        out_ref[1] = late_ref[...]

    @pl.when(step + 8 >= limit)
    def _():
        out_ref[1] = jnp.zeros(out_ref.shape[1:], BF16)


def early_call(counts, edge, latent, halo, late, tw, tb, sw, sb):
    frames, rows, cols, width = latent.shape
    wide = sw.shape[3]
    whole = lambda a: pl.BlockSpec(a.shape, lambda l, j: (0,) * a.ndim)
    out = pl.pallas_call(
        early_kernel,
        grid=(2, 4),
        in_specs=[
            pl.BlockSpec(memory_space=pltpu.SMEM),
            whole(edge),
            pl.BlockSpec((2, rows, cols, width), lambda l, j: (0, 0, 0, 0)),
            whole(halo),
            pl.BlockSpec((1, rows, cols, wide), lambda l, j: (4 * l + j, 0, 0, 0)),
        ]
        + [whole(a) for a in (tw, tb, sw, sb)],
        out_specs=pl.BlockSpec((2, 1, rows, cols, wide), lambda l, j: (0, 4 * l + j, 0, 0, 0)),
        out_shape=jax.ShapeDtypeStruct((2, 8, rows, cols, wide), BF16),
        scratch_shapes=[
            pltpu.VMEM(((rows + 2) * cols, 3 * width), BF16),
            pltpu.VMEM(((rows + 2) * cols, width), BF16),
            pltpu.VMEM((3 * width, 2 * wide), BF16),
            pltpu.VMEM((4 * width, 2 * wide), BF16),
            pltpu.VMEM((rows, cols + 8, wide), F32),
            pltpu.VMEM((rows, cols + 8, wide), F32),
        ],
        compiler_params=pltpu.CompilerParams(
            dimension_semantics=("arbitrary", "arbitrary"), vmem_limit_bytes=LIMIT
        ),
        cost_estimate=pl.CostEstimate(flops=18 * 10**9, bytes_accessed=20 * 10**6, transcendentals=5 * 10**6),
        name="early_frames",
    )(counts, edge, latent, halo, late, tw, tb, sw, sb)
    return out.reshape(16, rows, cols, wide)


def on_device(sizes, latent, temporal_weight, temporal_bias, spatial_weight, spatial_bias, counts):
    width = latent.shape[3]
    tw = temporal_weight.reshape(3 * width, 4 * width)
    args = (tw, temporal_bias.reshape(1, -1), spatial_weight, spatial_bias.reshape(1, -1))
    late, halo, edge = late_call(sizes, latent, *args)
    return early_call(counts, edge, latent, halo, late, *args)


def solution(mesh):
    sizes = (mesh.shape["fg"], mesh.shape["sp"])
    return jax.shard_map(
        functools.partial(on_device, sizes),
        mesh=mesh,
        in_specs=(P("fg", "sp", None, None), P(), P(), P(), P(), P()),
        out_specs=P("fg", "sp", None, None),
        check_vma=False,
    )
```

time: 341 us -> 83.7 us (0.25)
  matrix products: 218 us -> 0 us
  Pallas kernels: 0 us -> 82.6 us
  waiting for transfers between devices: 73.7 us -> 0 us
  other arithmetic: 18.8 us -> 0 us
  local copies, waits for them, and re-layouts: 17.2 us -> 0 us
  starting transfers between devices: 10.1 us -> 0 us
    dot_general x12 -> x0, matrix products: 218 us -> none  [the longest x9 162 us: spatial_taps(): jnp.einsum('fhwc,cd->fhwd', framed[:, dy:dy + rows, dx:dx + cols, :], spa...]
    pallas_call x0 -> x2, Pallas kernels: none -> 82.6 us  [the longest x1 41.7 us: early_call(): pl.pallas_call(early_kernel, grid=(2, 4), in_specs=[pl.BlockSpec(memory_s...]
    ppermute x3 -> x0, waiting for transfers between devices: 73.7 us -> none  [the longest x1 42.2 us: extended(): after = lax.ppermute(leading, axis, down)]
    concatenate x1 -> x0, other arithmetic: 17.5 us -> none  [extended(): x = jnp.concatenate([before, x, after], axis=dim)]
    ppermute x3 -> x0, starting transfers between devices: 10.1 us -> none  [the longest x1 3.7 us: shifted(): return lax.ppermute(x, axis, pairs)]
    convert_element_type x1 -> x0, local copies, waits for them, and re-layouts: 7.79 us -> none  [temporal_block(): jax.nn.silu(pre).astype(jnp.bfloat16)]
    slice x3 -> x0, local copies, waits for them, and re-layouts: 6.83 us -> none  [the longest x1 2.94 us: on_device(): edge = shifted(latent[local_frames - 2:], 'fg', 1)]
  transfers between devices with their start and end apart: 3 -> 0, of which waited for: 3 -> 0; matrix products, arithmetic and copies ran while one was open for 8% -> 0% of each run, Pallas kernels for 0% -> 0%
where the time goes in v1:
time: 83.7 us; the launch traced here: 82.6 us
  Pallas kernels  82.6 us (99%)
    pallas_call x1, Pallas kernels, early_call(): pl.pallas_call(early_kernel, grid=(2, 4), in_specs=[pl.BlockSpec(memory_s...  41.7 us
    pallas_call x1, Pallas kernels, late_call(): pl.pallas_call(functools.partial(late_kernel, sizes), in_specs=[hbm] + [v...  40.9 us

profile of v1, /device:TPU:25, one launch (start us, length us, event | category | flops | bytes accessed | tf_op | source)
XLA Modules:
  0.0 82.6 jit_solution(6233224750898775448)
XLA Ops:
  0.0 40.9 %late_frames.1 = (bf16[8,8,240,128]{3,2,1,0:T(8,128)(2,1)}, bf16[2,6,240,256]{3,2,1,0:T(8,128)(2,1)}, bf16[2,8,240,256]{3,2,1,0:T(8,128)(2,1)}) custom-call(bf16[4,8,240,256]{3,2,1,0:T(8,128)(2,1)} %latent_ref.3, bf16[768,1024]{1,0:T(8,128)(2,1)} %bitcast.4, f32[1,1024]{1,0:T(1,128)} %bitcast.6, bf16[3,3,256,128]{3,2,1,0:T(8,128)(2,1)} %sw_ref.3, ...), custom_call_target="tpu_custom_call" | custom-call | flops 17999998976 | bytes 16000000 | tf_op jit(solution)/shard_map/late_frames/pallas_call | solution.py:164
  40.9 41.7 %early_frames.1 = bf16[2,8,8,240,128]{4,3,2,1,0:T(8,128)(2,1)} custom-call(s32[4]{0:T(128)} %counts_ref.1, bf16[2,8,240,256]{3,2,1,0:T(8,128)(2,1)} %get-tuple-element.8.edge_ref, bf16[4,8,240,256]{3,2,1,0:T(8,128)(2,1)} %latent_ref.3, bf16[2,6,240,256]{3,2,1,0:T(8,128)(2,1)} %get-tuple-element.9.halo_ref, ...), custom_call_target="tpu_custom_call" | custom-call | flops 17999998976 | bytes 20000000 | tf_op jit(solution)/shard_map/early_frames/pallas_call | solution.py:261

commit v2 on v1

--- a/solution.py
+++ b/solution.py
@@ -45,7 +45,7 @@
     right[:, cols:cols + 8, :] = jnp.zeros((n, 8, wide), F32)
 
 
-def row_pair(row, cols, w01, w2, left, right, sb_ref, p):
+def row_pair(row, cols, w01, w2, left, mid, right, sb_ref, p):
     wide = sb_ref.shape[1]
     taps = [row(q) for q in range(4)]
     a = jnp.concatenate([jnp.concatenate(taps[h:h + 3], axis=1) for h in range(2)], axis=0)
@@ -55,13 +55,14 @@
     for h in range(2):
         left[2 * p + h, 8:8 + cols, :] = r[h * cols:(h + 1) * cols, :wide]
         right[2 * p + h, 0:cols, :] = s[:, h * wide:(h + 1) * wide]
-        middle = r[h * cols:(h + 1) * cols, wide:] + sb_ref[...]
-        rows.append((left[2 * p + h, 7:7 + cols, :] + middle + right[2 * p + h, 1:1 + cols, :]).astype(BF16))
+        mid[2 * p + h] = r[h * cols:(h + 1) * cols, wide:]
+        total = left[2 * p + h, 7:7 + cols, :] + mid[2 * p + h] + right[2 * p + h, 1:1 + cols, :] + sb_ref[...]
+        rows.append(total.astype(BF16))
     return rows
 
 
 def late_kernel(sizes, latent_ref, tw_ref, tb_ref, sw_ref, sb_ref, out_ref, halo_ref, edge_ref,
-                lat, up, w01, w2, w3, left, right, load_sem, send_sem, recv_sem):
+                lat, up, w01, w2, w3, left, mid, right, load_sem, send_sem, recv_sem):
     frames, rows, cols, width = latent_ref.shape
     wide = sb_ref.shape[1]
     fg, sp = lax.axis_index("fg"), lax.axis_index("sp")
@@ -110,11 +111,12 @@
 
     def inner(i, carry):
         l, j = i // 4, i % 4
-        a = jnp.concatenate([lat[l + k].reshape(rows * cols, width) for k in range(3)], axis=1)
-        up[i] = activation(a, j, tw_ref, tb_ref)
+        for t in range(0, rows, 2):
+            a = jnp.concatenate([lat[l + k, t:t + 2].reshape(2 * cols, width) for k in range(3)], axis=1)
+            up[i, t * cols:(t + 2) * cols, :] = activation(a, j, tw_ref, tb_ref)
         for p in range(rows // 2 - 1):
             row = lambda q: up[i, pl.ds((2 * p + q) * cols, cols), :]
-            for h, value in enumerate(row_pair(row, cols, w01, w2, left, right, sb_ref, p)):
+            for h, value in enumerate(row_pair(row, cols, w01, w2, left, mid, right, sb_ref, p)):
                 out_ref[i, 2 * p + 1 + h] = value
         return carry
 
@@ -177,6 +179,7 @@
             pltpu.VMEM((4 * width, 2 * wide), BF16),
             pltpu.VMEM((3 * width, 3 * wide), BF16),
             pltpu.VMEM((rows, cols + 8, wide), F32),
+            pltpu.VMEM((rows, cols, wide), F32),
             pltpu.VMEM((rows, cols + 8, wide), F32),
             pltpu.SemaphoreType.DMA((frames,)),
             pltpu.SemaphoreType.DMA((len(SENDS),)),
@@ -191,7 +194,7 @@
 
 
 def early_kernel(counts_ref, edge_ref, latent_ref, halo_ref, late_ref, tw_ref, tb_ref, sw_ref, sb_ref, out_ref,
-                 x_ref, up, w01, w2, left, right):
+                 x_ref, up, w01, w2, left, mid, right):
     rows, cols, width = latent_ref.shape[1:]
     fg, sp = lax.axis_index("fg"), lax.axis_index("sp")
     last_sp = lax.axis_size("sp") - 1
@@ -226,7 +229,9 @@
 
     @pl.when(valid)
     def _():
-        up[...] = activation(x_ref[...], j, tw_ref, tb_ref)
+        for t in range(0, rows + 2, 2):
+            at = pl.ds(t * cols, 2 * cols)
+            up[at, :] = activation(x_ref[at, :], j, tw_ref, tb_ref)
 
         @pl.when(sp == 0)
         def _():
@@ -238,7 +243,7 @@
 
         for p in range(rows // 2):
             row = lambda q: up[pl.ds((2 * p + q) * cols, cols), :]
-            for h, value in enumerate(row_pair(row, cols, w01, w2, left, right, sb_ref, p)):
+            for h, value in enumerate(row_pair(row, cols, w01, w2, left, mid, right, sb_ref, p)):
                 out_ref[0, 0, 2 * p + h] = value
 
     @pl.when(jnp.logical_not(valid))
@@ -277,6 +282,7 @@
             pltpu.VMEM((3 * width, 2 * wide), BF16),
             pltpu.VMEM((4 * width, 2 * wide), BF16),
             pltpu.VMEM((rows, cols + 8, wide), F32),
+            pltpu.VMEM((rows, cols, wide), F32),
             pltpu.VMEM((rows, cols + 8, wide), F32),
         ],
         compiler_params=pltpu.CompilerParams(

time: 83.7 us -> 72.4 us (0.86)
  the two profiles are of different devices: /device:TPU:25 before, /device:TPU:16 now
where the time goes in v2:
time: 72.4 us; the launch traced here: 72.1 us
  Pallas kernels  72 us (99%)
    pallas_call x1, Pallas kernels, late_call(): pl.pallas_call(functools.partial(late_kernel, sizes), in_specs=[hbm] + [v...  41.5 us
    pallas_call x1, Pallas kernels, early_call(): pl.pallas_call(early_kernel, grid=(2, 4), in_specs=[pl.BlockSpec(memory_s...  30.5 us

profile of v2, /device:TPU:16, one launch (start us, length us, event | category | flops | bytes accessed | tf_op | source)
XLA Modules:
  0.0 72.1 jit_solution(6126938203456015645)
XLA Ops:
  0.0 41.5 %late_frames.1 = (bf16[8,8,240,128]{3,2,1,0:T(8,128)(2,1)}, bf16[2,6,240,256]{3,2,1,0:T(8,128)(2,1)}, bf16[2,8,240,256]{3,2,1,0:T(8,128)(2,1)}) custom-call(bf16[4,8,240,256]{3,2,1,0:T(8,128)(2,1)} %latent_ref.3, bf16[768,1024]{1,0:T(8,128)(2,1)} %bitcast.4, f32[1,1024]{1,0:T(1,128)} %bitcast.6, bf16[3,3,256,128]{3,2,1,0:T(8,128)(2,1)} %sw_ref.3, ...), custom_call_target="tpu_custom_call" | custom-call | flops 17999998976 | bytes 16000000 | tf_op jit(solution)/shard_map/late_frames/pallas_call | solution.py:166
  41.5 30.5 %early_frames.1 = bf16[2,8,8,240,128]{4,3,2,1,0:T(8,128)(2,1)} custom-call(s32[4]{0:T(128)} %counts_ref.1, bf16[2,8,240,256]{3,2,1,0:T(8,128)(2,1)} %get-tuple-element.8.edge_ref, bf16[4,8,240,256]{3,2,1,0:T(8,128)(2,1)} %latent_ref.3, bf16[2,6,240,256]{3,2,1,0:T(8,128)(2,1)} %get-tuple-element.9.halo_ref, ...), custom_call_target="tpu_custom_call" | custom-call | flops 17999998976 | bytes 20000000 | tf_op jit(solution)/shard_map/early_frames/pallas_call | solution.py:266

commit v3 on v2

--- a/solution.py
+++ b/solution.py
@@ -96,8 +96,8 @@
             device_id=(fg + by[0], sp + by[1]), device_id_type=MESH,
         )
 
-    for i, by in enumerate(SENDS):
-        @pl.when(there(by))
+    for i in (4, 0, 1, 2, 3):
+        @pl.when(there(SENDS[i]))
         def _():
             sent(i).start()
 

time: 72.4 us -> 72.6 us (level)
  the two profiles are of different devices: /device:TPU:16 before, /device:TPU:25 now
where the time goes in v3:
time: 72.6 us; the launch traced here: 71.6 us
  Pallas kernels  71.6 us (99%)
    pallas_call x1, Pallas kernels, late_call(): pl.pallas_call(functools.partial(late_kernel, sizes), in_specs=[hbm] + [v...  41 us
    pallas_call x1, Pallas kernels, early_call(): pl.pallas_call(early_kernel, grid=(2, 4), in_specs=[pl.BlockSpec(memory_s...  30.6 us

profile of v3, /device:TPU:25, one launch (start us, length us, event | category | flops | bytes accessed | tf_op | source)
XLA Modules:
  0.0 71.6 jit_solution(2609977777514097995)
XLA Ops:
  0.0 41.0 %late_frames.1 = (bf16[8,8,240,128]{3,2,1,0:T(8,128)(2,1)}, bf16[2,6,240,256]{3,2,1,0:T(8,128)(2,1)}, bf16[2,8,240,256]{3,2,1,0:T(8,128)(2,1)}) custom-call(bf16[4,8,240,256]{3,2,1,0:T(8,128)(2,1)} %latent_ref.3, bf16[768,1024]{1,0:T(8,128)(2,1)} %bitcast.4, f32[1,1024]{1,0:T(1,128)} %bitcast.6, bf16[3,3,256,128]{3,2,1,0:T(8,128)(2,1)} %sw_ref.3, ...), custom_call_target="tpu_custom_call" | custom-call | flops 17999998976 | bytes 16000000 | tf_op jit(solution)/shard_map/late_frames/pallas_call | solution.py:166
  41.0 30.6 %early_frames.1 = bf16[2,8,8,240,128]{4,3,2,1,0:T(8,128)(2,1)} custom-call(s32[4]{0:T(128)} %counts_ref.1, bf16[2,8,240,256]{3,2,1,0:T(8,128)(2,1)} %get-tuple-element.8.edge_ref, bf16[4,8,240,256]{3,2,1,0:T(8,128)(2,1)} %latent_ref.3, bf16[2,6,240,256]{3,2,1,0:T(8,128)(2,1)} %get-tuple-element.9.halo_ref, ...), custom_call_target="tpu_custom_call" | custom-call | flops 17999998976 | bytes 20000000 | tf_op jit(solution)/shard_map/early_frames/pallas_call | solution.py:266
